TPU v7x, 128 devices: a whole 4x4x4 slice. The times are simulated.
128 devices in a mesh: role: 2 (over x_lo), vocab: 64 (over x_hi, y, z, core).
Axes of the slice: x: 4 (x_hi: 2, x_lo: 2; x = x_hi * 2 + x_lo), y: 4, z: 4, core: 2. Of those that a mesh axis runs over, the one named last changes fastest.
Arguments:
- teacher_rows: bfloat16 [1024, 4096], P(None, 'role'), may hold values from -256 to 256
- teacher_head: bfloat16 [4096, 81920], P('role', 'vocab'), may hold values from -4 to 4
- student_rows: bfloat16 [1024, 5120], P(None, 'role'), may hold values from -256 to 256
- student_head: bfloat16 [5120, 81920], P('role', 'vocab'), may hold values from -2 to 2
- token_ids: int32 [1024], replicated, may hold values from 0 to 81919
- loss_mask: int32 [1024], replicated, may hold values 0 or 1
Outputs:
- total_loss: float32 [], replicated
- weight_grad: bfloat16 [5120, 81920], P('role', 'vocab')
- hidden_grad: bfloat16 [1024, 5120], P('vocab', 'role')
All inputs are finite; a program needn't handle non-finite values.
Results may differ from a plain program's by a relative error of at most 0.0053.
Values may be sent and summed in bfloat16 or wider, within the bound.
A program may use at most 128 MiB of HBM per device.

v0:
```python
import jax
import jax.numpy as jnp
from jax import lax
from jax.sharding import PartitionSpec as P

TAU = 2.0
BETA = 0.5


def slab_stats(teacher_cool, student_logits, student_cool):
    teacher_top, student_top = lax.pmax(
        (jnp.max(teacher_cool, axis=1), jnp.max(student_logits, axis=1)), "vocab"
    )
    teacher_total, cooled_total, student_total = lax.psum(
        (
            jnp.sum(jnp.exp(teacher_cool - teacher_top[:, None]), axis=1),
            jnp.sum(jnp.exp(student_cool - (student_top / TAU)[:, None]), axis=1),
            jnp.sum(jnp.exp(student_logits - student_top[:, None]), axis=1),
        ),
        "vocab",
    )
    return (teacher_top, teacher_total, student_top, cooled_total, student_total)


def distill(teacher_sum, student_logits, label_ids, row_mask, slab_start):
    teacher_cool = teacher_sum / TAU
    student_cool = student_logits / TAU
    teacher_top, teacher_total, student_top, cooled_total, student_total = slab_stats(
        teacher_cool, student_logits, student_cool
    )
    teacher_log = teacher_cool - teacher_top[:, None] - jnp.log(teacher_total)[:, None]
    cooled_log = student_cool - (student_top / TAU)[:, None] - jnp.log(cooled_total)[:, None]
    student_log = student_logits - student_top[:, None] - jnp.log(student_total)[:, None]
    teacher_prob = jnp.exp(teacher_log)
    weight = row_mask.astype(jnp.float32)[:, None]
    columns = lax.broadcasted_iota(jnp.int32, student_logits.shape, 1) + slab_start
    picked = (columns == label_ids[:, None]).astype(jnp.float32)
    loss_part = jnp.sum(
        weight
        * (TAU * TAU * teacher_prob * (teacher_log - cooled_log) - BETA * picked * student_log)
    )
    gradient = (
        weight
        * (TAU * (jnp.exp(cooled_log) - teacher_prob) + BETA * (jnp.exp(student_log) - picked))
    ).astype(jnp.bfloat16)
    return (gradient, loss_part)


def shards(teacher_rows, teacher_head, student_rows, student_head, token_ids, loss_mask):
    slab_width = student_head.shape[1]
    slab_start = lax.axis_index("vocab") * slab_width
    teacher_part = jnp.dot(teacher_rows, teacher_head, preferred_element_type=jnp.float32)
    student_part = jnp.dot(student_rows, student_head, preferred_element_type=jnp.float32)
    teacher_sum, student_logits = lax.psum((teacher_part, student_part), "role")
    gradient, loss_part = distill(teacher_sum, student_logits, token_ids, loss_mask, slab_start)
    total_loss = lax.psum(loss_part, "vocab")
    weight_grad = lax.dot_general(
        student_rows, gradient, (((0,), (0,)), ((), ())), preferred_element_type=jnp.float32
    ).astype(jnp.bfloat16)
    hidden_grad = lax.psum_scatter(
        lax.dot_general(
            gradient, student_head, (((1,), (1,)), ((), ())), preferred_element_type=jnp.float32
        ),
        "vocab",
        scatter_dimension=0,
        tiled=True,
    ).astype(jnp.bfloat16)
    return (total_loss, weight_grad, hidden_grad)


def solution(mesh):
    placed = (P(None, "role"), P("role", "vocab"), P(None, "role"), P("role", "vocab"), P(), P())
    return jax.shard_map(
        shards,
        mesh=mesh,
        in_specs=placed,
        out_specs=(P(), P("role", "vocab"), P("vocab", "role")),
        check_vma=False,
    )
```

profile of v0, /device:TPU:0, one launch (start us, length us, event | category | flops | bytes accessed | tf_op | source)
XLA Modules:
  0.0 1162.3 jit_solution(17012144195760876278)
XLA Ops:
  7.2 0.0 all-reduce.5.cloned.1.call-start
  7.2 0.0 copy-start.2
  7.2 0.0 copy-start.3
  7.2 10.5 fusion.10
  17.7 0.0 copy-done.2
  17.7 0.0 copy-done.3
  17.7 8.6 fusion.11
  26.3 0.0 copy-start.1
  26.3 0.0 all-reduce.5.cloned.1.call-update
  26.4 0.0 reduce-scatter.2.cloned.1.call-start
  26.4 0.6 copy-done.1
  27.0 252.3 %all-reduce.5.cloned.1.call-done = (f32[1024,1280]{1,0:T(8,128)}, f32[1024,1280]{1,0:T(8,128)}) async-done(((f32[1024,1280]{1,0:T(8,128)}, f32[1024,1280]{1,0:T(8,128)}), (f32[1024,1280]{1,0:T(8,128)}, f32[1024,1280]{1,0:T(8,128)})) %all-reduce.5.cloned.1.call-update) | async-done | bytes 10485776 | tf_op jit(solution)/shard_map/psum | solution.py:54
  279.3 2.9 multiply_reduce_fusion
  282.2 2.8 reduce_max.19
  285.0 171.2 %all-reduce.1 = (f32[1024]{0:T(1024)S(1)}, f32[1024]{0:T(1024)S(1)}) all-reduce(f32[1024]{0:T(1024)S(1)} %reduce_max.19, f32[1024]{0:T(1024)S(1)} %multiply_reduce_fusion), channel_id=1, replica_groups=mesh['role'=2,'vocab'=64] {'vocab'}, use_global_device_ids=true, to_apply=%region_7.0 | all-reduce | flops 2048 | bytes 16384 | tf_op jit(solution)/shard_map/pmax | solution.py:11
  456.2 0.0 copy-start
  456.3 3.7 exponential_reduce_fusion.1
  460.0 3.5 exponential_reduce_fusion.2
  463.5 323.1 %all-reduce = (f32[1024]{0:T(1024)S(1)}, f32[1024]{0:T(1024)S(1)}, f32[1024]{0:T(1024)S(1)}) all-reduce(f32[1024]{0:T(1024)S(1)} %get-tuple-element.7, f32[1024]{0:T(1024)S(1)} %get-tuple-element.6, f32[1024]{0:T(1024)S(1)} %exponential_reduce_fusion.2), channel_id=1, replica_groups=mesh['role'=2,'vocab'=64] {'vocab'}, use_global_device_ids=true, to_apply=%region_11.0 | all-reduce | flops 3072 | bytes 24576 | tf_op jit(solution)/shard_map/psum | solution.py:14
  786.6 0.0 copy-done
  786.6 11.3 fusion.9
  797.9 11.5 fusion.12
  809.4 0.0 reduce-scatter.2.cloned.1.call-update
  809.4 163.3 %psum.47 = f32[]{:T(128)} all-reduce(f32[]{:T(128)} %get-tuple-element.16), channel_id=1, replica_groups=mesh['role'=2,'vocab'=64] {'vocab'}, use_global_device_ids=true, to_apply=%region_13.0 | all-reduce | flops 1 | bytes 8 | tf_op jit(solution)/shard_map/psum | solution.py:56
  972.7 11.4 fusion
  984.2 9.5 copy.9
  993.7 160.3 %reduce-scatter.2.cloned.1.call-done = f32[16,2560]{1,0:T(8,128)} async-done(((f32[1024,2560]{1,0:T(8,128)}), f32[16,2560]{1,0:T(8,128)}) %reduce-scatter.2.cloned.1.call-update) | async-done | bytes 163856 | tf_op jit(solution)/shard_map/reduce_scatter | solution.py:60
  1153.9 1.6 convert_element_type.23
  (6 shorter events, 0.0 us)
Async XLA Ops:
  7.2 272.1 %all-reduce.5.cloned.1.call-start = ((), (), s32[]{:S(2)}) async-start(), calls=%async_computation.2 | async-start | bytes 20971520 | tf_op jit(solution)/shard_map/psum | solution.py:54
  7.2 10.5 copy-start.2
  7.2 10.5 copy-start.3
  26.3 0.7 copy-start.1
  26.4 1127.6 %reduce-scatter.2.cloned.1.call-start = ((), (), s32[]{:S(2)}) async-start(), calls=%async_computation.1 | async-start | bytes 10649600 | tf_op jit(solution)/shard_map/reduce_scatter | solution.py:60
  456.2 330.4 %copy-start = (s32[1024]{0:T(1024)S(1)}, s32[1024]{0:T(1024)}, u32[]{:S(2)}) copy-start(s32[1024]{0:T(1024)} %param.10) | copy-start | bytes 12292
Sparse Core Ops, SparseCore 0:
  26.5 252.7 all-reduce.4
  809.5 344.3 reduce-scatter.1
where the time goes:
time: 1160 us
  blocking collectives  658 us (57%)
  waiting for transfers between devices  413 us (36%)
  matrix products  42 us (4%)
  other arithmetic  25.8 us (2%)
  between operations  14.1 us (1%)
    psum x1, blocking collectives, slab_stats(): lax.psum((jnp.sum(jnp.exp(teacher_cool - teacher_top[:, None]), axis=1),...  323 us
    psum x1, waiting for transfers between devices, shards(): teacher_sum, student_logits = lax.psum((teacher_part, student_part), 'role')  252 us
    pmax x1, blocking collectives, slab_stats(): lax.pmax((jnp.max(teacher_cool, axis=1), jnp.max(student_logits, axis=1))...  171 us
    psum x1, blocking collectives, shards(): total_loss = lax.psum(loss_part, 'vocab')  163 us
    reduce_scatter x1, waiting for transfers between devices, shards(): lax.psum_scatter(lax.dot_general(gradient, student_head, (((1,), (1,)), (...  160 us
  transfers between devices with their start and end apart: 2, of which 2 were waited for; matrix products, arithmetic and copies ran while one was open for 2% of the time, Pallas kernels for 0%

commit v1 on v0

v1 whole, which is shorter than its diff:
```python
import functools

import jax
import jax.numpy as jnp
from jax import lax
from jax.experimental import pallas as pl
from jax.experimental.pallas import tpu as pltpu
from jax.sharding import PartitionSpec as P

TAU = 2.0
BETA = 0.5
MESH = pl.DeviceIdType.MESH
F32 = jnp.float32
BF16 = jnp.bfloat16

CHUNKS = 4
AHEAD = 2
TILE = 256
LEVELS = 32767.0
XH, Y, Z, CORES = 2, 4, 4, 2


def as_columns(rows_ref, columns_ref):
    columns_ref[...] = rows_ref[...].T


def stacked(rows):
    place = lax.broadcasted_iota(jnp.int32, (8, 128), 0)
    tile = jnp.zeros((8, 128), F32)
    for k, row in enumerate(rows):
        tile = jnp.where(place == k, row, tile)
    return tile


def merge(tiles):
    top_t = functools.reduce(jnp.maximum, [t[0:1] for t in tiles])
    top_s = functools.reduce(jnp.maximum, [t[1:2] for t in tiles])
    teacher = cooled = student = cross = picked = 0.0
    for t in tiles:
        down_t = t[0:1] - top_t
        down_s = (t[1:2] - top_s) * 0.5
        scale_t = jnp.exp(down_t)
        scale_s = jnp.exp(down_s)
        teacher = teacher + t[2:3] * scale_t
        cooled = cooled + t[3:4] * scale_s
        student = student + t[4:5] * (scale_s * scale_s)
        cross = cross + scale_t * (t[5:6] + (down_t - down_s) * t[2:3])
        picked = picked + t[6:7]
    return top_t, top_s, teacher, cooled, student, cross, picked


def kernel(
    ids_ref, mask_ref, trows_hbm, thead_hbm, srows_hbm, shead_hbm,
    loss_ref, wgrad_hbm, hgrad_ref,
    trows, thead, srows, shead, mine, theirs, qs, qr, scale_s, scale_r, scale_columns,
    pad, columns, stat_columns, st_z, st_y, st_c, st_x, grad, h32, h16, rc, z16, zr, yown, y16, yr, xown, x16, xr,
    wtile, loss_row, loss_all,
    load_sem, q_sem, scale_sem, stz_sem, sty_sem, stc_sem, stx_sem, grad_sem, core_sem, z_sem, y_send, y_recv, x_sem,
    loss_sem, out_sem,
):
    r = lax.axis_index("role")
    v = lax.axis_index("vocab")
    core, z, y, xh = v % CORES, (v // 2) % Z, (v // 8) % Y, v // 32
    half = mine.shape[2]
    width = mine.shape[3]
    chunk = 2 * half
    model = shead.shape[0]
    tiles = width // TILE
    slab_start = v * width

    def at(role=r, x_hi=xh, yy=y, zz=z, cc=core):
        return (role, ((x_hi * Y + yy) * Z + zz) * CORES + cc)

    partner = at(role=1 - r)
    other_core = at(cc=1 - core)
    other_x = at(x_hi=1 - xh)

    def z_peer(k):
        return at(zz=(z + k) % Z)

    def y_peer(k):
        return at(yy=(y + k) % Y)

    def remote(src, dst, send, recv, device):
        return pltpu.make_async_remote_copy(
            src_ref=src, dst_ref=dst, send_sem=send, recv_sem=recv, device_id=device, device_id_type=MESH
        )

    sent = []

    def load_rows(m, first):
        hbm, ref = ((trows_hbm, trows), (srows_hbm, srows))[m]
        part = pl.ds(0, chunk) if first else pl.ds(chunk, ref.shape[0] - chunk)
        return pltpu.make_async_copy(hbm.at[part], ref.at[part], load_sem.at[m, tiles + (0 if first else 1)])

    def load_head(m, n):
        hbm, ref = ((thead_hbm, thead), (shead_hbm, shead))[m]
        part = pl.ds(pl.multiple_of(n * TILE, TILE), TILE)
        return pltpu.make_async_copy(hbm.at[:, part], ref.at[:, part], load_sem.at[m, n])

    for m in range(2):
        load_rows(m, True).start()
        for n in range(tiles):
            load_head(m, n).start()
    for m in range(2):
        load_rows(m, False).start()

    barrier = pltpu.get_barrier_semaphore()
    peers = [partner, other_core, other_x] + [z_peer(k) for k in (1, 2, 3)] + [y_peer(k) for k in (1, 2, 3)]
    for peer in peers:
        pl.semaphore_signal(barrier, inc=1, device_id=peer, device_id_type=MESH)

    pad[...] = jnp.zeros_like(pad)
    scale_columns[...] = jnp.zeros_like(scale_columns)
    stat_columns[...] = jnp.zeros_like(stat_columns)
    loss_row[...] = jnp.zeros_like(loss_row)

    def q_copy(c, m):
        return remote(qs.at[c, m], qr.at[c, m], q_sem.at[0, c, m], q_sem.at[1, c, m], partner)

    def scale_copy(c):
        return remote(scale_s.at[c], scale_r.at[c], scale_sem.at[0, c], scale_sem.at[1, c], partner)

    def logits(c):
        for m, (rows, head) in enumerate(((trows, thead), (srows, shead))):
            if c < 2:
                load_rows(m, c == 0).wait()

            @pl.loop(0, tiles)
            def _(n):
                if c == 0:
                    load_head(m, n).wait()
                part = pl.ds(pl.multiple_of(n * TILE, TILE), TILE)
                product = jnp.dot(rows[pl.ds(c * chunk, chunk), :], head[:, part], preferred_element_type=F32)
                low, high = product[:half], product[half:]
                mine[c, m, :, part] = jnp.where(r == 0, low, high)
                theirs[m, :, part] = jnp.where(r == 0, high, low)

            @pl.loop(0, half // 16)
            def _(b):
                part = pl.ds(pl.multiple_of(b * 16, 16), 16)
                x = theirs[m, part, :]
                top = jnp.maximum(jnp.max(jnp.abs(x), axis=1, keepdims=True), 1e-30)
                qs[c, m, part, :] = jnp.round(x * (LEVELS / top)).astype(jnp.int32).astype(jnp.int16)
                scale_columns[part, m : m + 1] = top * (1.0 / LEVELS)

            if c == 0 and m == 0:
                pl.semaphore_wait(barrier, len(peers))
            q_copy(c, m).start()
            sent.append(q_copy(c, m))
        scale_s[c] = scale_columns[...].T[0:8]
        scale_copy(c).start()
        sent.append(scale_copy(c))

    def spread(ref, sems, c, me, peer):
        copies = [
            remote(ref.at[c, me], ref.at[c, me], sems.at[0, c, k], sems.at[1, c, k], d) for k, d in enumerate(peer)
        ]
        for copy in copies:
            copy.start()
        sent.extend(copies)
        return copies

    def joined(ref, c, copies):
        for copy in copies:
            copy.wait_recv()
        return merge([ref[c, i] for i in range(ref.shape[1])])

    def local_stats(c):
        scale_copy(c).wait_recv()
        for m in range(2):
            q_copy(c, m).wait_recv()
        pad[0:8, :] = scale_r[c]
        pad[8:9, :] = ids_ref[pl.ds(2 * c + r, 1), :].astype(F32)
        as_columns(pad, columns)

        @pl.loop(0, half // 16)
        def _(b):
            part = pl.ds(pl.multiple_of(b * 16, 16), 16)
            got_t = qr[c, 0, part, :].astype(jnp.int32).astype(F32) * columns[part, 0:1]
            got_s = qr[c, 1, part, :].astype(jnp.int32).astype(F32) * columns[part, 1:2]
            t = (mine[c, 0, part, :] + got_t) * (1.0 / TAU)
            s = mine[c, 1, part, :] + got_s
            label = columns[part, 8:9].astype(jnp.int32)
            place = lax.broadcasted_iota(jnp.int32, s.shape, 1) + slab_start
            top_t = jnp.max(t, axis=1, keepdims=True)
            top_s = jnp.max(s, axis=1, keepdims=True)
            down_t = t - top_t
            down_s = (s - top_s) * (1.0 / TAU)
            exp_t = jnp.exp(down_t)
            exp_s = jnp.exp(down_s)
            mine[c, 0, part, :] = exp_t
            mine[c, 1, part, :] = exp_s
            sums = (
                top_t,
                top_s,
                jnp.sum(exp_t, axis=1, keepdims=True),
                jnp.sum(exp_s, axis=1, keepdims=True),
                jnp.sum(exp_s * exp_s, axis=1, keepdims=True),
                jnp.sum(exp_t * (down_t - down_s), axis=1, keepdims=True),
                jnp.sum(jnp.where(place == label, s, 0.0), axis=1, keepdims=True),
            )
            for k, value in enumerate(sums):
                stat_columns[part, k : k + 1] = value

        tile = stat_columns[...].T[0:8]
        st_z[c, z] = tile
        return tile[0:1], tile[1:2], spread(st_z, stz_sem, c, z, [z_peer(k) for k in (1, 2, 3)])

    def grad_copy(c, h):
        block = grad.at[2 * c + h]
        return remote(block, block, grad_sem.at[0, c], grad_sem.at[1, c], partner)

    def gradient(c, own_t, own_s, stats):
        top_t, top_s, teacher, cooled, student, cross, picked = stats
        mask = mask_ref[pl.ds(2 * c + r, 1), :].astype(F32)
        down_s = jnp.exp((own_s - top_s) * 0.5)
        pad[0:8, :] = stacked([
            TAU * mask * (down_s / cooled),
            TAU * mask * (jnp.exp(own_t - top_t) / teacher),
            BETA * mask * (down_s * down_s / student),
            BETA * mask,
        ])
        as_columns(pad, columns)
        loss_row[...] += mask * (
            TAU * TAU * (cross / teacher - jnp.log(teacher) + jnp.log(cooled))
            - BETA * (picked - top_s - jnp.log(student))
        )

        @pl.loop(0, half // 16)
        def _(b):
            part = pl.ds(pl.multiple_of(b * 16, 16), 16)
            exp_t = mine[c, 0, part, :]
            exp_s = mine[c, 1, part, :]
            label = columns[part, 8:9].astype(jnp.int32)
            place = lax.broadcasted_iota(jnp.int32, exp_s.shape, 1) + slab_start
            g = exp_s * (columns[part, 0:1] + columns[part, 2:3] * exp_s) - exp_t * columns[part, 1:2]
            g = g - jnp.where(place == label, columns[part, 3:4], 0.0)
            grad[2 * c + r, part, :] = g.astype(BF16)

        grad_copy(c, r).start()
        sent.append(grad_copy(c, r))

    def core_copy(g, slot):
        return remote(h16.at[slot, :, 1 - core], rc.at[g], core_sem.at[0, g], core_sem.at[1, g], other_core)

    def z_copies(g, slot):
        return [
            remote(z16.at[slot, (z + k) % Z], zr.at[g, k - 1], z_sem.at[0, g, k - 1], z_sem.at[1, g, k - 1], z_peer(k))
            for k in (1, 2, 3)
        ]

    def y_copy(g):
        hop = (g % Y - y + Y) % Y
        return remote(y16.at[g], yr.at[g // Y, hop - 1], y_send.at[g], y_recv.at[g // Y, hop - 1], at(yy=g % Y))

    x_copy = remote(x16, xr, x_sem.at[0], x_sem.at[1], other_x)
    busy = {}

    def hidden(c, h, slot):
        g = 2 * c + h
        for copy in busy.pop(("core", slot), []):
            copy.wait_send()

        @pl.loop(0, model // 512)
        def _(n):
            part = pl.ds(pl.multiple_of(n * 512, 512), 512)
            product = lax.dot_general(
                grad[g], shead[part, :], (((1,), (1,)), ((), ())), preferred_element_type=F32
            ).reshape(Z, CORES, 16, 512)
            h32[slot, :, :, :, part] = product
            h16[slot, :, :, :, part] = product.astype(BF16)

        core_copy(g, slot).start()
        busy["core", slot] = [core_copy(g, slot)]

    def over_z(c, h, slot):
        g = 2 * c + h
        core_copy(g, slot).wait_recv()
        for copy in busy.pop(("z", slot), []):
            copy.wait_send()

        @pl.loop(0, Z)
        def _(i):
            total = h32[slot, i, core] + rc[g, i].astype(F32)
            h32[slot, i, core] = total
            z16[slot, i] = total.astype(BF16)

        for copy in z_copies(g, slot):
            copy.start()
        busy["z", slot] = z_copies(g, slot)

    def over_y(c, h, slot):
        g = 2 * c + h
        for copy in z_copies(g, slot):
            copy.wait_recv()
        total = h32[slot, z, core]
        for k in range(Z - 1):
            total = total + zr[g, k].astype(F32)
        y16[g] = total.astype(BF16)

        @pl.when(y == g % Y)
        def _():
            yown[g // Y] = total

        @pl.when(y != g % Y)
        def _():
            y_copy(g).start()

    def over_x(c, h):
        g = 2 * c + h

        @pl.when(y == g % Y)
        def _():
            total = yown[g // Y]
            for k in range(Y - 1):
                remote(
                    y16.at[g], yr.at[g // Y, k], y_send.at[g], y_recv.at[g // Y, k], partner
                ).wait_recv()
            for k in range(Y - 1):
                total = total + yr[g // Y, k].astype(F32)

            @pl.when(xh == g // Y)
            def _():
                xown[...] = total

            @pl.when(xh != g // Y)
            def _():
                x16[...] = total.astype(BF16)
                x_copy.start()

    def weight_tiles(first, last):
        @pl.loop(first, last)
        def _(f):
            part = pl.ds(pl.multiple_of(f * TILE, TILE), TILE)
            product = lax.dot_general(
                srows[:, part], grad[...].reshape(2 * CHUNKS * half, width),
                (((0,), (0,)), ((), ())), preferred_element_type=F32,
            )
            wtile[f] = product.astype(BF16)
            pltpu.make_async_copy(wtile.at[f], wgrad_hbm.at[part], out_sem.at[f]).start()

    own, other = r, 1 - r
    for c in range(AHEAD):
        logits(c)
    for c in range(CHUNKS):
        own_t, own_s, copies = local_stats(c)
        if c + AHEAD < CHUNKS:
            logits(c + AHEAD)
        st_y[c, y] = stacked(joined(st_z, c, copies))
        copies = spread(st_y, sty_sem, c, y, [y_peer(k) for k in (1, 2, 3)])
        if c > 0:
            hidden(c - 1, own, 0)
        st_c[c, core] = stacked(joined(st_y, c, copies))
        copies = spread(st_c, stc_sem, c, core, [other_core])
        if c > 0:
            grad_copy(c - 1, other).wait_recv()
            hidden(c - 1, other, 1)
        st_x[c, xh] = stacked(joined(st_c, c, copies))
        copies = spread(st_x, stx_sem, c, xh, [other_x])
        if c > 0:
            over_z(c - 1, own, 0)
            over_z(c - 1, other, 1)
        gradient(c, own_t, own_s, joined(st_x, c, copies))
        if c > 0:
            over_y(c - 1, own, 0)
            over_y(c - 1, other, 1)
            over_x(c - 1, own)
            over_x(c - 1, other)

    last = CHUNKS - 1
    loss_all[r] = jnp.broadcast_to(loss_row[...], (8, 128))
    loss_copy = remote(loss_all.at[r], loss_all.at[r], loss_sem.at[0], loss_sem.at[1], partner)
    loss_copy.start()
    hidden(last, own, 0)
    over_z(last, own, 0)
    over_y(last, own, 0)
    grad_copy(last, other).wait_recv()
    hidden(last, other, 1)
    n_f = model // TILE
    weight_tiles(0, 3)
    over_z(last, other, 1)
    over_x(last, own)
    weight_tiles(3, 6)
    over_y(last, other, 1)
    weight_tiles(6, 8)
    over_x(last, other)
    weight_tiles(8, n_f)
    x_copy.wait_recv()
    hgrad_ref[...] = (xown[...] + xr[...].astype(F32)).astype(BF16)
    loss_copy.wait_recv()
    loss_ref[...] = jnp.sum(loss_all[0, 0:1, :] + loss_all[1, 0:1, :], axis=1, keepdims=True)

    loss_copy.wait_send()
    x_copy.wait_send()
    for copies in busy.values():
        for copy in copies:
            copy.wait_send()
    for copy in sent:
        copy.wait_send()
    for g in range(2 * CHUNKS):
        @pl.when(y != g % Y)
        def _():
            y_copy(g).wait_send()

    @pl.loop(0, n_f)
    def _(f):
        part = pl.ds(pl.multiple_of(f * TILE, TILE), TILE)
        pltpu.make_async_copy(wtile.at[f], wgrad_hbm.at[part], out_sem.at[f]).wait()


def shards(teacher_rows, teacher_head, student_rows, student_head, token_ids, loss_mask):
    tokens, d_t = teacher_rows.shape
    d_s, width = student_head.shape
    half = tokens // (2 * CHUNKS)
    blocks = 2 * CHUNKS
    vmem = pl.BlockSpec(memory_space=pltpu.VMEM)
    anywhere = pl.BlockSpec(memory_space=pl.ANY)
    dma = pltpu.SemaphoreType.DMA
    tiles = width // TILE
    loss, wgrad, hgrad = pl.pallas_call(
        kernel,
        out_shape=(
            jax.ShapeDtypeStruct((1, 1), F32),
            jax.ShapeDtypeStruct((d_s, width), BF16),
            jax.ShapeDtypeStruct((16, d_s), BF16),
        ),
        in_specs=[vmem, vmem, anywhere, anywhere, anywhere, anywhere],
        out_specs=(vmem, anywhere, vmem),
        scratch_shapes=[
            pltpu.VMEM((tokens, d_t), BF16),
            pltpu.VMEM((d_t, width), BF16),
            pltpu.VMEM((tokens, d_s), BF16),
            pltpu.VMEM((d_s, width), BF16),
            pltpu.VMEM((CHUNKS, 2, half, width), F32),
            pltpu.VMEM((2, half, width), F32),
            pltpu.VMEM((CHUNKS, 2, half, width), jnp.int16),
            pltpu.VMEM((CHUNKS, 2, half, width), jnp.int16),
            pltpu.VMEM((CHUNKS, 8, 128), F32),
            pltpu.VMEM((CHUNKS, 8, 128), F32),
            pltpu.VMEM((128, 128), F32),
            pltpu.VMEM((128, 128), F32),
            pltpu.VMEM((128, 128), F32),
            pltpu.VMEM((128, 128), F32),
            pltpu.VMEM((CHUNKS, Z, 8, 128), F32),
            pltpu.VMEM((CHUNKS, Y, 8, 128), F32),
            pltpu.VMEM((CHUNKS, CORES, 8, 128), F32),
            pltpu.VMEM((CHUNKS, XH, 8, 128), F32),
            pltpu.VMEM((blocks, half, width), BF16),
            pltpu.VMEM((2, Z, CORES, 16, d_s), F32),
            pltpu.VMEM((2, Z, CORES, 16, d_s), BF16),
            pltpu.VMEM((blocks, Z, 16, d_s), BF16),
            pltpu.VMEM((2, Z, 16, d_s), BF16),
            pltpu.VMEM((blocks, Z - 1, 16, d_s), BF16),
            pltpu.VMEM((XH, 16, d_s), F32),
            pltpu.VMEM((blocks, 16, d_s), BF16),
            pltpu.VMEM((XH, Y - 1, 16, d_s), BF16),
            pltpu.VMEM((16, d_s), F32),
            pltpu.VMEM((16, d_s), BF16),
            pltpu.VMEM((16, d_s), BF16),
            pltpu.VMEM((d_s // TILE, TILE, width), BF16),
            pltpu.VMEM((1, 128), F32),
            pltpu.VMEM((2, 8, 128), F32),
            dma((2, tiles + 2)),
            dma((2, CHUNKS, 2)),
            dma((2, CHUNKS)),
            dma((2, CHUNKS, Z - 1)),
            dma((2, CHUNKS, Y - 1)),
            dma((2, CHUNKS, CORES - 1)),
            dma((2, CHUNKS, XH - 1)),
            dma((2, CHUNKS)),
            dma((2, blocks)),
            dma((2, blocks, Z - 1)),
            dma((blocks,)),
            dma((XH, Y - 1)),
            dma((2,)),
            dma((2,)),
            dma((d_s // TILE,)),
        ],
        compiler_params=pltpu.CompilerParams(
            collective_id=0, has_side_effects=True, vmem_limit_bytes=60 << 20
        ),
        cost_estimate=pl.CostEstimate(flops=26_000_000_000, bytes_accessed=28_000_000, transcendentals=2_000_000),
        name="distill",
    )(
        token_ids.reshape(tokens // 128, 128),
        loss_mask.reshape(tokens // 128, 128),
        teacher_rows,
        teacher_head,
        student_rows,
        student_head,
    )
    return loss.reshape(()), wgrad, hgrad


def solution(mesh):
    placed = (P(None, "role"), P("role", "vocab"), P(None, "role"), P("role", "vocab"), P(), P())
    return jax.shard_map(
        shards,
        mesh=mesh,
        in_specs=placed,
        out_specs=(P(), P("role", "vocab"), P("vocab", "role")),
        check_vma=False,
    )
```

time: 1160 us -> 175 us (0.15)
  the two profiles are of different devices: /device:TPU:0 before, /device:TPU:22 now
where the time goes in v1:
time: 175 us
  Pallas kernels  165 us (94%)
  local copies, waits for them, and re-layouts  6.74 us (4%)
  between operations  2.45 us (1%)
    pallas_call x1, Pallas kernels, shards(): pl.pallas_call(kernel, out_shape=(jax.ShapeDtypeStruct((1, 1), F32), jax....  165 us
    unnamed x4, local copies, waits for them, and re-layouts  6.74 us

profile of v1, /device:TPU:22, one launch (start us, length us, event | category | flops | bytes accessed | tf_op | source)
XLA Modules:
  0.0 174.5 jit_solution(3424011998407509873)
XLA Ops:
  0.6 165.3 %distill.1 = (f32[1,1]{1,0:T(1,128)}, bf16[2560,1280]{1,0:T(8,128)(2,1)}, bf16[16,2560]{1,0:T(8,128)(2,1)}) custom-call(s32[8,128]{1,0:T(8,128)} %bitcast.3, s32[8,128]{1,0:T(8,128)} %bitcast.4, bf16[1024,2048]{1,0:T(8,128)(2,1)} %trows_hbm.1, bf16[2048,1280]{1,0:T(8,128)(2,1)} %thead_hbm.1, bf16[1024,2560]{1,0:T(8,128)(2,1)} %srows_hbm.1, ...), custom_call_target="tpu_custom_call" | custom-call | flops 25999998976 | bytes 28000000 | tf_op jit(solution)/shard_map/distill/pallas_call | solution.py:421
  166.6 0.0 copy-start
  166.7 6.1 %copy.13 = bf16[2560,1280]{1,0:T(8,128)(2,1)} copy(bf16[2560,1280]{1,0:T(8,128)(2,1)} %get-tuple-element.13) | data formatting | bytes 13107200
  172.8 0.0 copy-done
  172.8 0.6 copy.14
Async XLA Ops:
  166.6 6.1 %copy-start = (bf16[16,2560]{1,0:T(8,128)(2,1)S(1)}, bf16[16,2560]{1,0:T(8,128)(2,1)}, u32[]{:S(2)}) copy-start(bf16[16,2560]{1,0:T(8,128)(2,1)} %get-tuple-element.14) | copy-start | bytes 245764

commit v2 on v1

--- a/solution.py
+++ b/solution.py
@@ -18,6 +18,10 @@
 TILE = 256
 LEVELS = 32767.0
 XH, Y, Z, CORES = 2, 4, 4, 2
+SLOTS = 3
+PARTS = 2
+HIDDEN_TILE = 640
+W_SLOTS = 5
 
 
 def as_columns(rows_ref, columns_ref):
@@ -74,6 +78,8 @@
     partner = at(role=1 - r)
     other_core = at(cc=1 - core)
     other_x = at(x_hi=1 - xh)
+    side = (r + xh) % 2
+    facing = at(role=1 - r, x_hi=1 - xh)
 
     def z_peer(k):
         return at(zz=(z + k) % Z)
@@ -106,7 +112,7 @@
         load_rows(m, False).start()
 
     barrier = pltpu.get_barrier_semaphore()
-    peers = [partner, other_core, other_x] + [z_peer(k) for k in (1, 2, 3)] + [y_peer(k) for k in (1, 2, 3)]
+    peers = [partner, other_core, other_x, facing] + [z_peer(k) for k in (1, 2, 3)] + [y_peer(k) for k in (1, 2, 3)]
     for peer in peers:
         pl.semaphore_signal(barrier, inc=1, device_id=peer, device_id_type=MESH)
 
@@ -133,8 +139,8 @@
                 part = pl.ds(pl.multiple_of(n * TILE, TILE), TILE)
                 product = jnp.dot(rows[pl.ds(c * chunk, chunk), :], head[:, part], preferred_element_type=F32)
                 low, high = product[:half], product[half:]
-                mine[c, m, :, part] = jnp.where(r == 0, low, high)
-                theirs[m, :, part] = jnp.where(r == 0, high, low)
+                mine[c, m, :, part] = jnp.where(side == 0, low, high)
+                theirs[m, :, part] = jnp.where(side == 0, high, low)
 
             @pl.loop(0, half // 16)
             def _(b):
@@ -171,7 +177,7 @@
         for m in range(2):
             q_copy(c, m).wait_recv()
         pad[0:8, :] = scale_r[c]
-        pad[8:9, :] = ids_ref[pl.ds(2 * c + r, 1), :].astype(F32)
+        pad[8:9, :] = ids_ref[pl.ds(2 * c + side, 1), :].astype(F32)
         as_columns(pad, columns)
 
         @pl.loop(0, half // 16)
@@ -213,7 +219,7 @@
 
     def gradient(c, own_t, own_s, stats):
         top_t, top_s, teacher, cooled, student, cross, picked = stats
-        mask = mask_ref[pl.ds(2 * c + r, 1), :].astype(F32)
+        mask = mask_ref[pl.ds(2 * c + side, 1), :].astype(F32)
         down_s = jnp.exp((own_s - top_s) * 0.5)
         pad[0:8, :] = stacked([
             TAU * mask * (down_s / cooled),
@@ -236,177 +242,237 @@
             place = lax.broadcasted_iota(jnp.int32, exp_s.shape, 1) + slab_start
             g = exp_s * (columns[part, 0:1] + columns[part, 2:3] * exp_s) - exp_t * columns[part, 1:2]
             g = g - jnp.where(place == label, columns[part, 3:4], 0.0)
-            grad[2 * c + r, part, :] = g.astype(BF16)
-
-        grad_copy(c, r).start()
-        sent.append(grad_copy(c, r))
-
-    def core_copy(g, slot):
-        return remote(h16.at[slot, :, 1 - core], rc.at[g], core_sem.at[0, g], core_sem.at[1, g], other_core)
-
-    def z_copies(g, slot):
+            grad[2 * c + side, part, :] = g.astype(BF16)
+
+        grad_copy(c, side).start()
+        sent.append(grad_copy(c, side))
+
+    def span(p):
+        return pl.ds(p * (model // PARTS), model // PARTS)
+
+    def slot_of(c, h):
+        return 2 * (c % SLOTS) + h
+
+    def core_copy(c, h, p):
+        g = 2 * c + h
+        return remote(
+            h16.at[slot_of(c, h), :, :, span(p)], rc.at[g, :, :, span(p)],
+            core_sem.at[0, g, p], core_sem.at[1, g, p], other_core,
+        )
+
+    def z_copies(c, h, p):
+        g = 2 * c + h
         return [
-            remote(z16.at[slot, (z + k) % Z], zr.at[g, k - 1], z_sem.at[0, g, k - 1], z_sem.at[1, g, k - 1], z_peer(k))
+            remote(
+                z16.at[slot_of(c, h), (z + k) % Z, :, span(p)], zr.at[g, k - 1, :, span(p)],
+                z_sem.at[0, g, p, k - 1], z_sem.at[1, g, p, k - 1], z_peer(k),
+            )
             for k in (1, 2, 3)
         ]
 
-    def y_copy(g):
+    def y_copy(g, p):
         hop = (g % Y - y + Y) % Y
-        return remote(y16.at[g], yr.at[g // Y, hop - 1], y_send.at[g], y_recv.at[g // Y, hop - 1], at(yy=g % Y))
-
-    x_copy = remote(x16, xr, x_sem.at[0], x_sem.at[1], other_x)
-    busy = {}
-
-    def hidden(c, h, slot):
+        return remote(
+            y16.at[g, :, span(p)], yr.at[g // Y, hop - 1, :, span(p)],
+            y_send.at[g, p], y_recv.at[g // Y, hop - 1, p], at(yy=g % Y),
+        )
+
+    def x_copy(p):
+        return remote(x16.at[:, span(p)], xr.at[:, span(p)], x_sem.at[0, p], x_sem.at[1, p], other_x)
+
+    def hidden(c, h, count):
         g = 2 * c + h
-        for copy in busy.pop(("core", slot), []):
-            copy.wait_send()
-
-        @pl.loop(0, model // 512)
-        def _(n):
-            part = pl.ds(pl.multiple_of(n * 512, 512), 512)
-            product = lax.dot_general(
-                grad[g], shead[part, :], (((1,), (1,)), ((), ())), preferred_element_type=F32
-            ).reshape(Z, CORES, 16, 512)
-            h32[slot, :, :, :, part] = product
-            h16[slot, :, :, :, part] = product.astype(BF16)
-
-        core_copy(g, slot).start()
-        busy["core", slot] = [core_copy(g, slot)]
-
-    def over_z(c, h, slot):
+        if c >= SLOTS:
+            for i in range(count):
+                for p in range(PARTS):
+                    core_copy(c - SLOTS, h + i, p).wait_send()
+        wide = HIDDEN_TILE
+        for p in range(PARTS):
+            @pl.loop(0, model // PARTS // wide)
+            def _(n):
+                part = pl.ds(pl.multiple_of(p * (model // PARTS) + n * wide, 128), wide)
+                product = lax.dot_general(
+                    grad[pl.ds(g, count)].reshape(count * half, width), shead[part, :],
+                    (((1,), (1,)), ((), ())), preferred_element_type=F32,
+                ).reshape(count, Z, CORES, 16, wide)
+                for i in range(count):
+                    first, second = product[i, :, 0], product[i, :, 1]
+                    slot = slot_of(c, h) + i
+                    h32[slot, :, :, part] = jnp.where(core == 0, first, second)
+                    h16[slot, :, :, part] = jnp.where(core == 0, second, first).astype(BF16)
+
+            for i in range(count):
+                core_copy(c, h + i, p).start()
+
+    def over_z(c, h):
         g = 2 * c + h
-        core_copy(g, slot).wait_recv()
-        for copy in busy.pop(("z", slot), []):
-            copy.wait_send()
-
-        @pl.loop(0, Z)
-        def _(i):
-            total = h32[slot, i, core] + rc[g, i].astype(F32)
-            h32[slot, i, core] = total
-            z16[slot, i] = total.astype(BF16)
-
-        for copy in z_copies(g, slot):
-            copy.start()
-        busy["z", slot] = z_copies(g, slot)
-
-    def over_y(c, h, slot):
+        slot = slot_of(c, h)
+        for p in range(PARTS):
+            core_copy(c, h, p).wait_recv()
+            if c >= SLOTS:
+                for copy in z_copies(c - SLOTS, h, p):
+                    copy.wait_send()
+
+            @pl.loop(0, Z)
+            def _(i):
+                total = h32[slot, i, :, span(p)] + rc[g, i, :, span(p)].astype(F32)
+                h32[slot, i, :, span(p)] = total
+                z16[slot, i, :, span(p)] = total.astype(BF16)
+
+            for copy in z_copies(c, h, p):
+                copy.start()
+
+    def over_y(c, h):
         g = 2 * c + h
-        for copy in z_copies(g, slot):
-            copy.wait_recv()
-        total = h32[slot, z, core]
-        for k in range(Z - 1):
-            total = total + zr[g, k].astype(F32)
-        y16[g] = total.astype(BF16)
+        for p in range(PARTS):
+            for copy in z_copies(c, h, p):
+                copy.wait_recv()
+            total = h32[slot_of(c, h), z, :, span(p)]
+            for k in range(Z - 1):
+                total = total + zr[g, k, :, span(p)].astype(F32)
+            y16[g, :, span(p)] = total.astype(BF16)
+
+            @pl.when(y == g % Y)
+            def _():
+                yown[g // Y, :, span(p)] = total
+
+            @pl.when(y != g % Y)
+            def _():
+                y_copy(g, p).start()
+
+    def over_x(c, h):
+        g = 2 * c + h
 
         @pl.when(y == g % Y)
         def _():
-            yown[g // Y] = total
-
-        @pl.when(y != g % Y)
-        def _():
-            y_copy(g).start()
-
-    def over_x(c, h):
-        g = 2 * c + h
-
-        @pl.when(y == g % Y)
-        def _():
-            total = yown[g // Y]
-            for k in range(Y - 1):
-                remote(
-                    y16.at[g], yr.at[g // Y, k], y_send.at[g], y_recv.at[g // Y, k], partner
-                ).wait_recv()
-            for k in range(Y - 1):
-                total = total + yr[g // Y, k].astype(F32)
-
-            @pl.when(xh == g // Y)
-            def _():
-                xown[...] = total
-
-            @pl.when(xh != g // Y)
-            def _():
-                x16[...] = total.astype(BF16)
-                x_copy.start()
+            for p in range(PARTS):
+                total = yown[g // Y, :, span(p)]
+                for k in range(Y - 1):
+                    remote(
+                        y16.at[g, :, span(p)], yr.at[g // Y, k, :, span(p)],
+                        y_send.at[g, p], y_recv.at[g // Y, k, p], partner,
+                    ).wait_recv()
+                for k in range(Y - 1):
+                    total = total + yr[g // Y, k, :, span(p)].astype(F32)
+
+                @pl.when(xh == g // Y)
+                def _():
+                    xown[:, span(p)] = total
+
+                @pl.when(xh != g // Y)
+                def _():
+                    x16[:, span(p)] = total.astype(BF16)
+                    x_copy(p).start()
+
+    def weight_copy(f):
+        part = pl.ds(pl.multiple_of(f * TILE, TILE), TILE)
+        return pltpu.make_async_copy(wtile.at[lax.rem(f, W_SLOTS)], wgrad_hbm.at[part], out_sem.at[lax.rem(f, W_SLOTS)])
 
     def weight_tiles(first, last):
         @pl.loop(first, last)
         def _(f):
+            @pl.when(f >= W_SLOTS)
+            def _():
+                weight_copy(f - W_SLOTS).wait()
+
             part = pl.ds(pl.multiple_of(f * TILE, TILE), TILE)
             product = lax.dot_general(
                 srows[:, part], grad[...].reshape(2 * CHUNKS * half, width),
                 (((0,), (0,)), ((), ())), preferred_element_type=F32,
             )
-            wtile[f] = product.astype(BF16)
-            pltpu.make_async_copy(wtile.at[f], wgrad_hbm.at[part], out_sem.at[f]).start()
-
-    own, other = r, 1 - r
+            wtile[lax.rem(f, W_SLOTS)] = product.astype(BF16)
+            weight_copy(f).start()
+
+    own, other = side, 1 - side
+
+    def both(stage, c):
+        stage(c, own)
+        stage(c, other)
+
+    def gap(step, place):
+        if place == 0 and step + AHEAD < CHUNKS:
+            logits(step + AHEAD)
+        if step == 2:
+            if place == 2:
+                grad_copy(0, other).wait_recv()
+                hidden(0, 0, 2)
+            if place == 3:
+                both(over_z, 0)
+        if step == 3:
+            if place == 0:
+                both(over_y, 0)
+            if place == 1:
+                both(over_x, 0)
+            if place == 2:
+                grad_copy(1, other).wait_recv()
+                hidden(1, 0, 2)
+            if place == 3:
+                both(over_z, 1)
+
     for c in range(AHEAD):
         logits(c)
     for c in range(CHUNKS):
         own_t, own_s, copies = local_stats(c)
-        if c + AHEAD < CHUNKS:
-            logits(c + AHEAD)
+        gap(c, 0)
         st_y[c, y] = stacked(joined(st_z, c, copies))
         copies = spread(st_y, sty_sem, c, y, [y_peer(k) for k in (1, 2, 3)])
-        if c > 0:
-            hidden(c - 1, own, 0)
+        gap(c, 1)
         st_c[c, core] = stacked(joined(st_y, c, copies))
         copies = spread(st_c, stc_sem, c, core, [other_core])
-        if c > 0:
-            grad_copy(c - 1, other).wait_recv()
-            hidden(c - 1, other, 1)
+        gap(c, 2)
         st_x[c, xh] = stacked(joined(st_c, c, copies))
-        copies = spread(st_x, stx_sem, c, xh, [other_x])
-        if c > 0:
-            over_z(c - 1, own, 0)
-            over_z(c - 1, other, 1)
+        copies = spread(st_x, stx_sem, c, xh, [facing])
+        gap(c, 3)
         gradient(c, own_t, own_s, joined(st_x, c, copies))
-        if c > 0:
-            over_y(c - 1, own, 0)
-            over_y(c - 1, other, 1)
-            over_x(c - 1, own)
-            over_x(c - 1, other)
-
-    last = CHUNKS - 1
-    loss_all[r] = jnp.broadcast_to(loss_row[...], (8, 128))
-    loss_copy = remote(loss_all.at[r], loss_all.at[r], loss_sem.at[0], loss_sem.at[1], partner)
+
+    loss_all[side] = jnp.broadcast_to(loss_row[...], (8, 128))
+    loss_copy = remote(loss_all.at[side], loss_all.at[side], loss_sem.at[0], loss_sem.at[1], partner)
     loss_copy.start()
-    hidden(last, own, 0)
-    over_z(last, own, 0)
-    over_y(last, own, 0)
-    grad_copy(last, other).wait_recv()
-    hidden(last, other, 1)
     n_f = model // TILE
-    weight_tiles(0, 3)
-    over_z(last, other, 1)
-    over_x(last, own)
-    weight_tiles(3, 6)
-    over_y(last, other, 1)
-    weight_tiles(6, 8)
-    over_x(last, other)
-    weight_tiles(8, n_f)
-    x_copy.wait_recv()
+    grad_copy(2, other).wait_recv()
+    hidden(2, 0, 2)
+    both(over_y, 1)
+    hidden(3, own, 1)
+    both(over_z, 2)
+    both(over_x, 1)
+    over_z(3, own)
+    both(over_y, 2)
+    grad_copy(3, other).wait_recv()
+    hidden(3, other, 1)
+    over_y(3, own)
+    weight_tiles(0, 2)
+    over_z(3, other)
+    both(over_x, 2)
+    over_x(3, own)
+    weight_tiles(2, 6)
+    over_y(3, other)
+    weight_tiles(6, n_f)
+    over_x(3, other)
+    for p in range(PARTS):
+        x_copy(p).wait_recv()
     hgrad_ref[...] = (xown[...] + xr[...].astype(F32)).astype(BF16)
     loss_copy.wait_recv()
     loss_ref[...] = jnp.sum(loss_all[0, 0:1, :] + loss_all[1, 0:1, :], axis=1, keepdims=True)
 
     loss_copy.wait_send()
-    x_copy.wait_send()
-    for copies in busy.values():
-        for copy in copies:
-            copy.wait_send()
     for copy in sent:
         copy.wait_send()
-    for g in range(2 * CHUNKS):
-        @pl.when(y != g % Y)
-        def _():
-            y_copy(g).wait_send()
-
-    @pl.loop(0, n_f)
+    for p in range(PARTS):
+        x_copy(p).wait_send()
+        for c in range(CHUNKS - SLOTS, CHUNKS):
+            for h in range(2):
+                core_copy(c, h, p).wait_send()
+                for copy in z_copies(c, h, p):
+                    copy.wait_send()
+
+        for g in range(2 * CHUNKS):
+            @pl.when(y != g % Y)
+            def _():
+                y_copy(g, p).wait_send()
+
+    @pl.loop(n_f - W_SLOTS, n_f)
     def _(f):
-        part = pl.ds(pl.multiple_of(f * TILE, TILE), TILE)
-        pltpu.make_async_copy(wtile.at[f], wgrad_hbm.at[part], out_sem.at[f]).wait()
+        weight_copy(f).wait()
 
 
 def shards(teacher_rows, teacher_head, student_rows, student_head, token_ids, loss_mask):
@@ -447,10 +513,10 @@
             pltpu.VMEM((CHUNKS, CORES, 8, 128), F32),
             pltpu.VMEM((CHUNKS, XH, 8, 128), F32),
             pltpu.VMEM((blocks, half, width), BF16),
-            pltpu.VMEM((2, Z, CORES, 16, d_s), F32),
-            pltpu.VMEM((2, Z, CORES, 16, d_s), BF16),
+            pltpu.VMEM((2 * SLOTS, Z, 16, d_s), F32),
+            pltpu.VMEM((2 * SLOTS, Z, 16, d_s), BF16),
             pltpu.VMEM((blocks, Z, 16, d_s), BF16),
-            pltpu.VMEM((2, Z, 16, d_s), BF16),
+            pltpu.VMEM((2 * SLOTS, Z, 16, d_s), BF16),
             pltpu.VMEM((blocks, Z - 1, 16, d_s), BF16),
             pltpu.VMEM((XH, 16, d_s), F32),
             pltpu.VMEM((blocks, 16, d_s), BF16),
@@ -458,7 +524,7 @@
             pltpu.VMEM((16, d_s), F32),
             pltpu.VMEM((16, d_s), BF16),
             pltpu.VMEM((16, d_s), BF16),
-            pltpu.VMEM((d_s // TILE, TILE, width), BF16),
+            pltpu.VMEM((W_SLOTS, TILE, width), BF16),
             pltpu.VMEM((1, 128), F32),
             pltpu.VMEM((2, 8, 128), F32),
             dma((2, tiles + 2)),
@@ -469,13 +535,13 @@
             dma((2, CHUNKS, CORES - 1)),
             dma((2, CHUNKS, XH - 1)),
             dma((2, CHUNKS)),
-            dma((2, blocks)),
-            dma((2, blocks, Z - 1)),
-            dma((blocks,)),
-            dma((XH, Y - 1)),
+            dma((2, blocks, PARTS)),
+            dma((2, blocks, PARTS, Z - 1)),
+            dma((blocks, PARTS)),
+            dma((XH, Y - 1, PARTS)),
+            dma((2, PARTS)),
             dma((2,)),
-            dma((2,)),
-            dma((d_s // TILE,)),
+            dma((W_SLOTS,)),
         ],
         compiler_params=pltpu.CompilerParams(
             collective_id=0, has_side_effects=True, vmem_limit_bytes=60 << 20

time: 175 us -> 139 us (0.79)
  Pallas kernels: 165 us -> 130 us
    pallas_call x1, Pallas kernels: 165 us -> 130 us  [shards(): pl.pallas_call(kernel, out_shape=(jax.ShapeDtypeStruct((1, 1), F32), jax....]
where the time goes in v2:
time: 139 us
  Pallas kernels  130 us (94%)
  local copies, waits for them, and re-layouts  6.74 us (5%)
  between operations  2.45 us (2%)
    pallas_call x1, Pallas kernels, shards(): pl.pallas_call(kernel, out_shape=(jax.ShapeDtypeStruct((1, 1), F32), jax....  130 us
    unnamed x4, local copies, waits for them, and re-layouts  6.74 us

profile of v2, /device:TPU:22, one launch (start us, length us, event | category | flops | bytes accessed | tf_op | source)
XLA Modules:
  0.0 139.2 jit_solution(5026053529292537465)
XLA Ops:
  0.6 130.0 %distill.1 = (f32[1,1]{1,0:T(1,128)}, bf16[2560,1280]{1,0:T(8,128)(2,1)}, bf16[16,2560]{1,0:T(8,128)(2,1)}) custom-call(s32[8,128]{1,0:T(8,128)} %bitcast.3, s32[8,128]{1,0:T(8,128)} %bitcast.4, bf16[1024,2048]{1,0:T(8,128)(2,1)} %trows_hbm.1, bf16[2048,1280]{1,0:T(8,128)(2,1)} %thead_hbm.1, bf16[1024,2560]{1,0:T(8,128)(2,1)} %srows_hbm.1, ...), custom_call_target="tpu_custom_call" | custom-call | flops 25999998976 | bytes 28000000 | tf_op jit(solution)/shard_map/distill/pallas_call | solution.py:487
  131.3 0.0 copy-start
  131.3 6.1 %copy.13 = bf16[2560,1280]{1,0:T(8,128)(2,1)} copy(bf16[2560,1280]{1,0:T(8,128)(2,1)} %get-tuple-element.13) | data formatting | bytes 13107200
  137.4 0.0 copy-done
  137.4 0.6 copy.14
Async XLA Ops:
  131.3 6.1 %copy-start = (bf16[16,2560]{1,0:T(8,128)(2,1)S(1)}, bf16[16,2560]{1,0:T(8,128)(2,1)}, u32[]{:S(2)}) copy-start(bf16[16,2560]{1,0:T(8,128)(2,1)} %get-tuple-element.14) | copy-start | bytes 245764

commit v3 on v2

--- a/solution.py
+++ b/solution.py
@@ -22,6 +22,7 @@
 PARTS = 2
 HIDDEN_TILE = 640
 W_SLOTS = 5
+CARRY = 10
 
 
 def as_columns(rows_ref, columns_ref):
@@ -104,12 +105,9 @@
         part = pl.ds(pl.multiple_of(n * TILE, TILE), TILE)
         return pltpu.make_async_copy(hbm.at[:, part], ref.at[:, part], load_sem.at[m, n])
 
-    for m in range(2):
-        load_rows(m, True).start()
-        for n in range(tiles):
-            load_head(m, n).start()
-    for m in range(2):
-        load_rows(m, False).start()
+    load_rows(0, True).start()
+    for n in range(tiles):
+        load_head(0, n).start()
 
     barrier = pltpu.get_barrier_semaphore()
     peers = [partner, other_core, other_x, facing] + [z_peer(k) for k in (1, 2, 3)] + [y_peer(k) for k in (1, 2, 3)]
@@ -132,10 +130,15 @@
             if c < 2:
                 load_rows(m, c == 0).wait()
 
+            if c == 0 and m == 0:
+                load_rows(1, True).start()
+
             @pl.loop(0, tiles)
             def _(n):
                 if c == 0:
                     load_head(m, n).wait()
+                    if m == 0:
+                        load_head(1, n).start()
                 part = pl.ds(pl.multiple_of(n * TILE, TILE), TILE)
                 product = jnp.dot(rows[pl.ds(c * chunk, chunk), :], head[:, part], preferred_element_type=F32)
                 low, high = product[:half], product[half:]
@@ -151,6 +154,8 @@
                 scale_columns[part, m : m + 1] = top * (1.0 / LEVELS)
 
             if c == 0 and m == 0:
+                for k in range(2):
+                    load_rows(k, False).start()
                 pl.semaphore_wait(barrier, len(peers))
             q_copy(c, m).start()
             sent.append(q_copy(c, m))
@@ -280,29 +285,29 @@
     def x_copy(p):
         return remote(x16.at[:, span(p)], xr.at[:, span(p)], x_sem.at[0, p], x_sem.at[1, p], other_x)
 
-    def hidden(c, h, count):
-        g = 2 * c + h
-        if c >= SLOTS:
-            for i in range(count):
+    def hidden(*blocks):
+        count = len(blocks)
+        for c, h in blocks:
+            if c >= SLOTS:
                 for p in range(PARTS):
-                    core_copy(c - SLOTS, h + i, p).wait_send()
+                    core_copy(c - SLOTS, h, p).wait_send()
         wide = HIDDEN_TILE
         for p in range(PARTS):
             @pl.loop(0, model // PARTS // wide)
             def _(n):
                 part = pl.ds(pl.multiple_of(p * (model // PARTS) + n * wide, 128), wide)
+                rows = [grad[2 * c + h] for c, h in blocks]
                 product = lax.dot_general(
-                    grad[pl.ds(g, count)].reshape(count * half, width), shead[part, :],
+                    rows[0] if count == 1 else jnp.concatenate(rows), shead[part, :],
                     (((1,), (1,)), ((), ())), preferred_element_type=F32,
                 ).reshape(count, Z, CORES, 16, wide)
-                for i in range(count):
+                for i, (c, h) in enumerate(blocks):
                     first, second = product[i, :, 0], product[i, :, 1]
-                    slot = slot_of(c, h) + i
-                    h32[slot, :, :, part] = jnp.where(core == 0, first, second)
-                    h16[slot, :, :, part] = jnp.where(core == 0, second, first).astype(BF16)
-
-            for i in range(count):
-                core_copy(c, h + i, p).start()
+                    h32[slot_of(c, h), :, :, part] = jnp.where(core == 0, first, second)
+                    h16[slot_of(c, h), :, :, part] = jnp.where(core == 0, second, first).astype(BF16)
+
+            for c, h in blocks:
+                core_copy(c, h, p).start()
 
     def over_z(c, h):
         g = 2 * c + h
@@ -368,6 +373,20 @@
         part = pl.ds(pl.multiple_of(f * TILE, TILE), TILE)
         return pltpu.make_async_copy(wtile.at[lax.rem(f, W_SLOTS)], wgrad_hbm.at[part], out_sem.at[lax.rem(f, W_SLOTS)])
 
+    early = 2 * (CHUNKS - 1)
+
+    def weight_sum(f, first, last):
+        part = pl.ds(pl.multiple_of(f * TILE, TILE), TILE)
+        return lax.dot_general(
+            srows[first * half : last * half, part], grad[first:last].reshape((last - first) * half, width),
+            (((0,), (0,)), ((), ())), preferred_element_type=F32,
+        )
+
+    def weight_ahead():
+        @pl.loop(0, CHUNKS)
+        def _(f):
+            mine[f] = weight_sum(f, 0, early).reshape(2, half, width)
+
     def weight_tiles(first, last):
         @pl.loop(first, last)
         def _(f):
@@ -375,12 +394,11 @@
             def _():
                 weight_copy(f - W_SLOTS).wait()
 
-            part = pl.ds(pl.multiple_of(f * TILE, TILE), TILE)
-            product = lax.dot_general(
-                srows[:, part], grad[...].reshape(2 * CHUNKS * half, width),
-                (((0,), (0,)), ((), ())), preferred_element_type=F32,
-            )
-            wtile[lax.rem(f, W_SLOTS)] = product.astype(BF16)
+            if first < CHUNKS:
+                total = mine[f].reshape(TILE, width) + weight_sum(f, early, 2 * CHUNKS)
+            else:
+                total = weight_sum(f, 0, 2 * CHUNKS)
+            wtile[lax.rem(f, W_SLOTS)] = total.astype(BF16)
             weight_copy(f).start()
 
     own, other = side, 1 - side
@@ -392,22 +410,30 @@
     def gap(step, place):
         if place == 0 and step + AHEAD < CHUNKS:
             logits(step + AHEAD)
-        if step == 2:
-            if place == 2:
-                grad_copy(0, other).wait_recv()
-                hidden(0, 0, 2)
-            if place == 3:
-                both(over_z, 0)
-        if step == 3:
-            if place == 0:
-                both(over_y, 0)
-            if place == 1:
-                both(over_x, 0)
-            if place == 2:
-                grad_copy(1, other).wait_recv()
-                hidden(1, 0, 2)
-            if place == 3:
-                both(over_z, 1)
+        if (step, place) == (1, 1):
+            hidden((0, own))
+        if (step, place) == (1, 3):
+            over_z(0, own)
+        if (step, place) == (2, 0):
+            hidden((1, own))
+        if (step, place) == (2, 1):
+            over_y(0, own)
+            over_z(1, own)
+        if (step, place) == (2, 3):
+            grad_copy(0, other).wait_recv()
+            hidden((0, other))
+        if (step, place) == (2, 4):
+            over_z(0, other)
+            hidden((2, own))
+            over_y(1, own)
+            over_z(2, own)
+        if (step, place) == (3, 0):
+            over_y(0, other)
+        if (step, place) == (3, 1):
+            over_y(2, own)
+        if (step, place) == (3, 3):
+            grad_copy(1, other).wait_recv()
+            hidden((1, other))
 
     for c in range(AHEAD):
         logits(c)
@@ -424,30 +450,33 @@
         copies = spread(st_x, stx_sem, c, xh, [facing])
         gap(c, 3)
         gradient(c, own_t, own_s, joined(st_x, c, copies))
+        gap(c, 4)
 
     loss_all[side] = jnp.broadcast_to(loss_row[...], (8, 128))
     loss_copy = remote(loss_all.at[side], loss_all.at[side], loss_sem.at[0], loss_sem.at[1], partner)
     loss_copy.start()
     n_f = model // TILE
+    over_z(1, other)
+    hidden((3, own))
     grad_copy(2, other).wait_recv()
-    hidden(2, 0, 2)
-    both(over_y, 1)
-    hidden(3, own, 1)
-    both(over_z, 2)
-    both(over_x, 1)
+    hidden((2, other))
     over_z(3, own)
-    both(over_y, 2)
+    over_y(1, other)
+    over_z(2, other)
+    weight_ahead()
     grad_copy(3, other).wait_recv()
-    hidden(3, other, 1)
+    hidden((3, other))
     over_y(3, own)
-    weight_tiles(0, 2)
     over_z(3, other)
-    both(over_x, 2)
+    over_y(2, other)
+    weight_tiles(0, CHUNKS)
+    over_y(3, other)
+    for c in range(CHUNKS - 1):
+        both(over_x, c)
     over_x(3, own)
-    weight_tiles(2, 6)
-    over_y(3, other)
-    weight_tiles(6, n_f)
+    weight_tiles(CHUNKS, 8)
     over_x(3, other)
+    weight_tiles(8, n_f)
     for p in range(PARTS):
         x_copy(p).wait_recv()
     hgrad_ref[...] = (xown[...] + xr[...].astype(F32)).astype(BF16)
@@ -473,6 +502,20 @@
     @pl.loop(n_f - W_SLOTS, n_f)
     def _(f):
         weight_copy(f).wait()
+
+
+def carry(src, dst, held, sems):
+    rows = src.shape[0] // CARRY
+    parts = [pl.ds(k * rows, rows) for k in range(CARRY)]
+    into = [pltpu.make_async_copy(src.at[p], held.at[p], sems.at[0, k]) for k, p in enumerate(parts)]
+    back = [pltpu.make_async_copy(held.at[p], dst.at[p], sems.at[1, k]) for k, p in enumerate(parts)]
+    for copy in into:
+        copy.start()
+    for first, second in zip(into, back):
+        first.wait()
+        second.start()
+    for copy in back:
+        copy.wait()
 
 
 def shards(teacher_rows, teacher_head, student_rows, student_head, token_ids, loss_mask):
@@ -556,6 +599,16 @@
         student_rows,
         student_head,
     )
+    wgrad = pl.pallas_call(
+        carry,
+        out_shape=jax.ShapeDtypeStruct(wgrad.shape, wgrad.dtype),
+        in_specs=[anywhere],
+        out_specs=anywhere,
+        scratch_shapes=[pltpu.VMEM(wgrad.shape, wgrad.dtype), dma((2, CARRY))],
+        compiler_params=pltpu.CompilerParams(vmem_limit_bytes=60 << 20),
+        cost_estimate=pl.CostEstimate(flops=0, bytes_accessed=2 * wgrad.size * 2, transcendentals=0),
+        name="carry",
+    )(wgrad)
     return loss.reshape(()), wgrad, hgrad
 
 

time: 139 us -> 130 us (0.935); the launches traced: 139 us -> 128 us
  local copies, waits for them, and re-layouts: 6.74 us -> 0.64 us
  Pallas kernels: 130 us -> 125 us
    pallas_call x1, Pallas kernels: 130 us -> 119 us  [shards(): pl.pallas_call(kernel, out_shape=(jax.ShapeDtypeStruct((1, 1), F32), jax....]
    unnamed x4 -> x3, local copies, waits for them, and re-layouts: 6.74 us -> 0.64 us
    pallas_call x0 -> x1, Pallas kernels: none -> 5.56 us  [shards(): pl.pallas_call(carry, out_shape=jax.ShapeDtypeStruct(wgrad.shape, wgrad.d...]
where the time goes in v3:
time: 130 us; the launch traced here: 128 us
  Pallas kernels  125 us (96%)
  between operations  2.47 us (2%)
    pallas_call x1, Pallas kernels, shards(): pl.pallas_call(kernel, out_shape=(jax.ShapeDtypeStruct((1, 1), F32), jax....  119 us
    pallas_call x1, Pallas kernels, shards(): pl.pallas_call(carry, out_shape=jax.ShapeDtypeStruct(wgrad.shape, wgrad.d...  5.56 us

profile of v3, /device:TPU:22, one launch (start us, length us, event | category | flops | bytes accessed | tf_op | source)
XLA Modules:
  0.0 128.0 jit_solution(17503920729006816727)
XLA Ops:
  0.6 119.4 %distill.1 = (f32[1,1]{1,0:T(1,128)}, bf16[2560,1280]{1,0:T(8,128)(2,1)}, bf16[16,2560]{1,0:T(8,128)(2,1)}) custom-call(s32[8,128]{1,0:T(8,128)} %bitcast.3, s32[8,128]{1,0:T(8,128)} %bitcast.4, bf16[1024,2048]{1,0:T(8,128)(2,1)} %trows_hbm.1, bf16[2048,1280]{1,0:T(8,128)(2,1)} %thead_hbm.1, bf16[1024,2560]{1,0:T(8,128)(2,1)} %srows_hbm.1, ...), custom_call_target="tpu_custom_call" | custom-call | flops 25999998976 | bytes 28000000 | tf_op jit(solution)/shard_map/distill/pallas_call | solution.py:530
  120.0 0.0 copy-start
  120.0 5.6 %carry.1 = bf16[2560,1280]{1,0:T(8,128)(2,1)} custom-call(bf16[2560,1280]{1,0:T(8,128)(2,1)} %get-tuple-element.7.src), custom_call_target="tpu_custom_call" | custom-call | bytes 13107200 | tf_op jit(solution)/shard_map/carry/pallas_call | solution.py:602
  126.3 0.0 copy-done
  126.3 0.6 copy.12
Async XLA Ops:
  120.0 6.3 %copy-start = (bf16[16,2560]{1,0:T(8,128)(2,1)S(1)}, bf16[16,2560]{1,0:T(8,128)(2,1)}, u32[]{:S(2)}) copy-start(bf16[16,2560]{1,0:T(8,128)(2,1)} %get-tuple-element.14) | copy-start | bytes 245764

commit v4 on v3

--- a/solution.py
+++ b/solution.py
@@ -20,8 +20,10 @@
 XH, Y, Z, CORES = 2, 4, 4, 2
 SLOTS = 3
 PARTS = 2
-HIDDEN_TILE = 640
-W_SLOTS = 5
+HIDDEN_TILE = 1280
+W_TILE = 512
+W_SLOTS = 3
+AHEAD_TILES = 2
 CARRY = 10
 
 
@@ -133,13 +135,15 @@
             if c == 0 and m == 0:
                 load_rows(1, True).start()
 
-            @pl.loop(0, tiles)
+            wide = TILE if c == 0 else width
+
+            @pl.loop(0, width // wide)
             def _(n):
                 if c == 0:
                     load_head(m, n).wait()
                     if m == 0:
                         load_head(1, n).start()
-                part = pl.ds(pl.multiple_of(n * TILE, TILE), TILE)
+                part = pl.ds(pl.multiple_of(n * wide, TILE), wide)
                 product = jnp.dot(rows[pl.ds(c * chunk, chunk), :], head[:, part], preferred_element_type=F32)
                 low, high = product[:half], product[half:]
                 mine[c, m, :, part] = jnp.where(side == 0, low, high)
@@ -369,23 +373,25 @@
                     x16[:, span(p)] = total.astype(BF16)
                     x_copy(p).start()
 
+    n_f = model // W_TILE
+    early = 2 * (CHUNKS - 1)
+    per_tile = W_TILE // (2 * half)
+
     def weight_copy(f):
-        part = pl.ds(pl.multiple_of(f * TILE, TILE), TILE)
+        part = pl.ds(pl.multiple_of(f * W_TILE, W_TILE), W_TILE)
         return pltpu.make_async_copy(wtile.at[lax.rem(f, W_SLOTS)], wgrad_hbm.at[part], out_sem.at[lax.rem(f, W_SLOTS)])
 
-    early = 2 * (CHUNKS - 1)
-
     def weight_sum(f, first, last):
-        part = pl.ds(pl.multiple_of(f * TILE, TILE), TILE)
+        part = pl.ds(pl.multiple_of(f * W_TILE, W_TILE), W_TILE)
         return lax.dot_general(
             srows[first * half : last * half, part], grad[first:last].reshape((last - first) * half, width),
             (((0,), (0,)), ((), ())), preferred_element_type=F32,
         )
 
     def weight_ahead():
-        @pl.loop(0, CHUNKS)
+        @pl.loop(0, AHEAD_TILES)
         def _(f):
-            mine[f] = weight_sum(f, 0, early).reshape(2, half, width)
+            mine[pl.ds(f * per_tile, per_tile)] = weight_sum(f, 0, early).reshape(per_tile, 2, half, width)
 
     def weight_tiles(first, last):
         @pl.loop(first, last)
@@ -394,8 +400,8 @@
             def _():
                 weight_copy(f - W_SLOTS).wait()
 
-            if first < CHUNKS:
-                total = mine[f].reshape(TILE, width) + weight_sum(f, early, 2 * CHUNKS)
+            if first < AHEAD_TILES:
+                total = mine[pl.ds(f * per_tile, per_tile)].reshape(W_TILE, width) + weight_sum(f, early, 2 * CHUNKS)
             else:
                 total = weight_sum(f, 0, 2 * CHUNKS)
             wtile[lax.rem(f, W_SLOTS)] = total.astype(BF16)
@@ -455,11 +461,9 @@
     loss_all[side] = jnp.broadcast_to(loss_row[...], (8, 128))
     loss_copy = remote(loss_all.at[side], loss_all.at[side], loss_sem.at[0], loss_sem.at[1], partner)
     loss_copy.start()
-    n_f = model // TILE
     over_z(1, other)
-    hidden((3, own))
     grad_copy(2, other).wait_recv()
-    hidden((2, other))
+    hidden((3, own), (2, other))
     over_z(3, own)
     over_y(1, other)
     over_z(2, other)
@@ -469,14 +473,14 @@
     over_y(3, own)
     over_z(3, other)
     over_y(2, other)
-    weight_tiles(0, CHUNKS)
+    weight_tiles(0, 2)
     over_y(3, other)
     for c in range(CHUNKS - 1):
         both(over_x, c)
     over_x(3, own)
-    weight_tiles(CHUNKS, 8)
+    weight_tiles(2, 4)
     over_x(3, other)
-    weight_tiles(8, n_f)
+    weight_tiles(4, n_f)
     for p in range(PARTS):
         x_copy(p).wait_recv()
     hgrad_ref[...] = (xown[...] + xr[...].astype(F32)).astype(BF16)
@@ -567,7 +571,7 @@
             pltpu.VMEM((16, d_s), F32),
             pltpu.VMEM((16, d_s), BF16),
             pltpu.VMEM((16, d_s), BF16),
-            pltpu.VMEM((W_SLOTS, TILE, width), BF16),
+            pltpu.VMEM((W_SLOTS, W_TILE, width), BF16),
             pltpu.VMEM((1, 128), F32),
             pltpu.VMEM((2, 8, 128), F32),
             dma((2, tiles + 2)),

time: 130 us -> 127 us (0.977)
  Pallas kernels: 125 us -> 123 us
    pallas_call x1, Pallas kernels: 119 us -> 118 us  [shards(): pl.pallas_call(kernel, out_shape=(jax.ShapeDtypeStruct((1, 1), F32), jax....]
where the time goes in v4:
time: 127 us; the launch traced here: 126 us
  Pallas kernels  123 us (97%)
  between operations  2.47 us (2%)
    pallas_call x1, Pallas kernels, shards(): pl.pallas_call(kernel, out_shape=(jax.ShapeDtypeStruct((1, 1), F32), jax....  118 us
    pallas_call x1, Pallas kernels, shards(): pl.pallas_call(carry, out_shape=jax.ShapeDtypeStruct(wgrad.shape, wgrad.d...  5.56 us

profile of v4, /device:TPU:22, one launch (start us, length us, event | category | flops | bytes accessed | tf_op | source)
XLA Modules:
  0.0 126.3 jit_solution(4177638228246584092)
XLA Ops:
  0.6 117.6 %distill.1 = (f32[1,1]{1,0:T(1,128)}, bf16[2560,1280]{1,0:T(8,128)(2,1)}, bf16[16,2560]{1,0:T(8,128)(2,1)}) custom-call(s32[8,128]{1,0:T(8,128)} %bitcast.3, s32[8,128]{1,0:T(8,128)} %bitcast.4, bf16[1024,2048]{1,0:T(8,128)(2,1)} %trows_hbm.1, bf16[2048,1280]{1,0:T(8,128)(2,1)} %thead_hbm.1, bf16[1024,2560]{1,0:T(8,128)(2,1)} %srows_hbm.1, ...), custom_call_target="tpu_custom_call" | custom-call | flops 25999998976 | bytes 28000000 | tf_op jit(solution)/shard_map/distill/pallas_call | solution.py:534
  118.3 0.0 copy-start
  118.3 5.6 %carry.1 = bf16[2560,1280]{1,0:T(8,128)(2,1)} custom-call(bf16[2560,1280]{1,0:T(8,128)(2,1)} %get-tuple-element.7.src), custom_call_target="tpu_custom_call" | custom-call | bytes 13107200 | tf_op jit(solution)/shard_map/carry/pallas_call | solution.py:606
  124.5 0.0 copy-done
  124.5 0.6 copy.12
Async XLA Ops:
  118.3 6.3 %copy-start = (bf16[16,2560]{1,0:T(8,128)(2,1)S(1)}, bf16[16,2560]{1,0:T(8,128)(2,1)}, u32[]{:S(2)}) copy-start(bf16[16,2560]{1,0:T(8,128)(2,1)} %get-tuple-element.14) | copy-start | bytes 245764

commit v5 on v4

--- a/solution.py
+++ b/solution.py
@@ -508,7 +508,10 @@
         weight_copy(f).wait()
 
 
-def carry(src, dst, held, sems):
+def carry(src, small_src, dst, small_dst, held, small_held, sems, small_sems):
+    small_into = pltpu.make_async_copy(small_src, small_held, small_sems.at[0])
+    small_back = pltpu.make_async_copy(small_held, small_dst, small_sems.at[1])
+    small_into.start()
     rows = src.shape[0] // CARRY
     parts = [pl.ds(k * rows, rows) for k in range(CARRY)]
     into = [pltpu.make_async_copy(src.at[p], held.at[p], sems.at[0, k]) for k, p in enumerate(parts)]
@@ -518,8 +521,11 @@
     for first, second in zip(into, back):
         first.wait()
         second.start()
+    small_into.wait()
+    small_back.start()
     for copy in back:
         copy.wait()
+    small_back.wait()
 
 
 def shards(teacher_rows, teacher_head, student_rows, student_head, token_ids, loss_mask):
@@ -603,16 +609,18 @@
         student_rows,
         student_head,
     )
-    wgrad = pl.pallas_call(
+    wgrad, hgrad = pl.pallas_call(
         carry,
-        out_shape=jax.ShapeDtypeStruct(wgrad.shape, wgrad.dtype),
-        in_specs=[anywhere],
-        out_specs=anywhere,
-        scratch_shapes=[pltpu.VMEM(wgrad.shape, wgrad.dtype), dma((2, CARRY))],
+        out_shape=tuple(jax.ShapeDtypeStruct(a.shape, a.dtype) for a in (wgrad, hgrad)),
+        in_specs=[anywhere, anywhere],
+        out_specs=(anywhere, anywhere),
+        scratch_shapes=[
+            pltpu.VMEM(wgrad.shape, wgrad.dtype), pltpu.VMEM(hgrad.shape, hgrad.dtype), dma((2, CARRY)), dma((2,)),
+        ],
         compiler_params=pltpu.CompilerParams(vmem_limit_bytes=60 << 20),
         cost_estimate=pl.CostEstimate(flops=0, bytes_accessed=2 * wgrad.size * 2, transcendentals=0),
         name="carry",
-    )(wgrad)
+    )(wgrad, hgrad)
     return loss.reshape(()), wgrad, hgrad
 
 

time: 127 us -> 127 us (level)
  no operation moved by 1% of the time
where the time goes in v5:
time: 127 us; the launch traced here: 126 us
  Pallas kernels  123 us (97%)
  between operations  2.45 us (2%)
    pallas_call x1, Pallas kernels, shards(): pl.pallas_call(kernel, out_shape=(jax.ShapeDtypeStruct((1, 1), F32), jax....  118 us
    pallas_call x1, Pallas kernels, shards(): pl.pallas_call(carry, out_shape=tuple((jax.ShapeDtypeStruct(a.shape, a.dt...  5.57 us

profile of v5, /device:TPU:22, one launch (start us, length us, event | category | flops | bytes accessed | tf_op | source)
XLA Modules:
  0.0 125.7 jit_solution(7977790368810750070)
XLA Ops:
  0.6 117.6 %distill.1 = (f32[1,1]{1,0:T(1,128)}, bf16[2560,1280]{1,0:T(8,128)(2,1)}, bf16[16,2560]{1,0:T(8,128)(2,1)}) custom-call(s32[8,128]{1,0:T(8,128)} %bitcast.3, s32[8,128]{1,0:T(8,128)} %bitcast.4, bf16[1024,2048]{1,0:T(8,128)(2,1)} %trows_hbm.1, bf16[2048,1280]{1,0:T(8,128)(2,1)} %thead_hbm.1, bf16[1024,2560]{1,0:T(8,128)(2,1)} %srows_hbm.1, ...), custom_call_target="tpu_custom_call" | custom-call | flops 25999998976 | bytes 28000000 | tf_op jit(solution)/shard_map/distill/pallas_call | solution.py:540
  118.3 5.6 %carry.1 = (bf16[2560,1280]{1,0:T(8,128)(2,1)}, bf16[16,2560]{1,0:T(8,128)(2,1)}) custom-call(bf16[2560,1280]{1,0:T(8,128)(2,1)} %get-tuple-element.9.src, bf16[16,2560]{1,0:T(8,128)(2,1)} %get-tuple-element.10.small_src), custom_call_target="tpu_custom_call" | custom-call | bytes 13107200 | tf_op jit(solution)/shard_map/carry/pallas_call | solution.py:612
